TPU v7x, 256 devices: a whole 4x4x8 slice. The times are simulated.
256 devices in a mesh: seq: 32 (over z, x), fsdp: 8 (over y, core).
Axes of the slice: x: 4, y: 4, z: 8, core: 2. Of those that a mesh axis runs over, the one named last changes fastest.
Arguments:
- query_in: bfloat16 [8, 4096, 5120], P('fsdp', 'seq'), may hold values from -400 to 400, as said below
- key_in: bfloat16 [8, 4096, 5120], P('fsdp', 'seq'), may hold values from -400 to 400
- value_in: bfloat16 [8, 4096, 5120], P('fsdp', 'seq'), may hold values from -24 to 24
- out_grad: bfloat16 [8, 4096, 5120], P('fsdp', 'seq'), may hold values from -24 to 24
- gain_q: bfloat16 [5120], P('fsdp'), may hold values from 0.099609375 to 1.8984375
- gain_k: bfloat16 [5120], P('fsdp'), may hold values from 0.099609375 to 1.8984375
- mask_lists: int32 [40, 32, 11], replicated, may hold values from 0 to 31, as said below
- tile_counts: int32 [40, 32], replicated, may hold values from 1 to 11
- head_slot: int32 [40], replicated, may hold values from 0 to 63, as said below
Outputs:
- attn_out: bfloat16 [8, 4096, 5120], P('fsdp', 'seq')
- lse_slots: float32 [8, 64, 4096], P('fsdp', 'seq')
- grad_q: bfloat16 [8, 4096, 5120], P('fsdp', 'seq')
- grad_k: bfloat16 [8, 4096, 5120], P('fsdp', 'seq')
- grad_v: bfloat16 [8, 4096, 5120], P('fsdp', 'seq')
- grad_gain_q: float32 [5120], P('fsdp')
- grad_gain_k: float32 [5120], P('fsdp')
Inputs may be any that keep to these rules, and one draw needn't show every extreme that they name: query_in and key_in are finite. `mask_lists`: for head h and query tile i, entries 0 to tile_counts[h, i] - 1 name distinct key tiles in increasing order, tile i among them; the entries after them are ignored. `head_slot`: the 40 heads have distinct slots; slot s belongs to the device of index s // 2 along seq; every device along seq holds between 1 and 2 heads, some device holding 2.
All inputs are finite; a program needn't handle non-finite values.
Results may differ from a plain program's by a relative error of at most 0.035.
The roundings to bfloat16 on the way count: a program that leaves them out, or rounds other values in their place, can miss the bound.
Values may be sent and summed in bfloat16 or wider, within the bound.
No kernel may reach another device: no remote copies, remote signals or barrier semaphores. Data moves between devices by JAX's collectives and lax.ppermute only.
A program may use at most 128 MiB of HBM per device.

v0:
```python
import functools
import math

import jax
import jax.numpy as jnp
from jax import lax
from jax.experimental import pallas as pl
from jax.experimental.pallas import tpu as pltpu
from jax.sharding import Mesh, PartitionSpec as P

norm_eps = 1e-06
head_width = 128
tile_rows = 128
block = (tile_rows, head_width)
log2e = 1.4426950408889634
ln2 = 0.6931471805599453
masked_out = -1e30
unrolled = 4
vmem_bytes = 26 * 2**20
most_vmem = 60 * 2**20

bf16 = jnp.bfloat16
f32 = jnp.float32
i32 = jnp.int32

vmem = pl.BlockSpec(memory_space=pltpu.VMEM)
smem = pl.BlockSpec(memory_space=pltpu.SMEM)
hbm = pl.BlockSpec(memory_space=pltpu.HBM)


def dot(a, b, contract):
    dims = ((contract[:1], contract[1:]), ((), ()))
    return lax.dot_general(a, b, dims, preferred_element_type=f32)


def staged(kernel, n_in, n_out, hbm_in, hbm_out, lazy, refs):
    ins, outs = list(refs[:n_in]), list(refs[n_in : n_in + n_out])
    rest = refs[n_in + n_out :]
    n_hbm = len(hbm_in) + len(hbm_out)
    scratch, buffers, sems = rest[: len(rest) - n_hbm - 1], rest[len(rest) - n_hbm - 1 : -1], rest[-1]
    reads, writes = {}, {}
    for c, i in enumerate(hbm_in):
        reads[i] = pltpu.make_async_copy(ins[i], buffers[c], sems.at[c])
        reads[i].start()
        ins[i] = buffers[c]
    for c, o in enumerate(hbm_out, len(hbm_in)):
        writes[o] = pltpu.make_async_copy(buffers[c], outs[o], sems.at[c])
        outs[o] = buffers[c]
    if lazy:
        kernel(*ins, *outs, *scratch, ready=lambda i: reads[i].wait(), flush=lambda o: writes[o].start())
    else:
        for i in hbm_in:
            reads[i].wait()
        kernel(*ins, *outs, *scratch)
        for o in hbm_out:
            writes[o].start()
    for o in hbm_out:
        writes[o].wait()


def call(kernel, name, outs, in_specs, tiles_moved, flops=0, scratch=(), smem_outs=(), hbm_in=(), hbm_out=(), lazy=False, room=vmem_bytes):
    def run(*operands):
        specs = [hbm if i in hbm_in else spec for i, spec in enumerate(in_specs)]
        kinds = (smem if n in smem_outs else hbm if n in hbm_out else vmem for n in range(len(outs)))
        buffers = [pltpu.VMEM(operands[i].shape, operands[i].dtype) for i in hbm_in]
        buffers += [pltpu.VMEM(*outs[o]) for o in hbm_out]
        body, extra = kernel, []
        if buffers:
            body = lambda *refs: staged(kernel, len(specs), len(outs), hbm_in, hbm_out, lazy, refs)
            extra = [*buffers, pltpu.SemaphoreType.DMA((len(buffers),))]
        return pl.pallas_call(
            body,
            out_shape=tuple(jax.ShapeDtypeStruct(*o) for o in outs),
            in_specs=specs,
            out_specs=tuple(kinds),
            scratch_shapes=[*scratch, *extra],
            compiler_params=pltpu.CompilerParams(
                vmem_limit_bytes=most_vmem if buffers else room
            ),
            cost_estimate=pl.CostEstimate(
                flops=flops, bytes_accessed=tiles_moved * tile_rows * head_width * 2, transcendentals=0
            ),
            name=name,
        )(*operands)

    return run


def cols(head):
    start = head * head_width
    if not isinstance(head, int):
        start = pl.multiple_of(start, head_width)
    return pl.ds(start, head_width)


def place_kernel(n_seq, heads, slot_ref, x_hbm, order_ref, main_hbm, held_ref, x_ref, read_sem, write_sems):
    read = pltpu.make_async_copy(x_hbm, x_ref, read_sem)
    read.start()

    @pl.loop(0, 2 * n_seq)
    def _(s):
        held_ref[s] = -1

    @pl.loop(0, heads)
    def _(h):
        held_ref[slot_ref[h]] = h

    def place(position, head):
        order_ref[position] = head
        order_ref[heads + head] = position

    def step(d, used):
        low, high = held_ref[2 * d], held_ref[2 * d + 1]
        place(d, jnp.where(low >= 0, low, high))
        both = jnp.logical_and(low >= 0, high >= 0)

        @pl.when(both)
        def _():
            place(used, high)

        return used + both.astype(i32)

    lax.fori_loop(0, n_seq, step, jnp.int32(n_seq))
    read.wait()
    writes = [
        pltpu.make_async_copy(x_ref.at[:, cols(order_ref[d])], main_hbm.at[d], write_sems.at[d])
        for d in range(n_seq)
    ]
    for write in writes:
        write.start()
    for write in writes:
        write.wait()


def norm_kernel(n_seq, heads, order_ref, q_ref, k_ref, v_ref, do_ref, gain_ref, kq_ref, grad_ref, extra_ref):
    for p in range(n_seq):
        grad_ref[p] = do_ref[:, cols(order_ref[p])]
    for which, x_ref in ((1, q_ref), (0, k_ref)):
        total = jnp.zeros(block, f32)
        for head in range(heads):
            x = x_ref[:, cols(head)].astype(f32)
            total += x * x
        mean = jnp.sum(total, axis=1, keepdims=True) * (1.0 / (heads * head_width))
        inverse = jnp.broadcast_to(lax.rsqrt(mean + norm_eps), block)
        for p in range(heads):
            at = cols(order_ref[p])
            gain = gain_ref[1 - which : 2 - which, at].astype(f32)
            normed = (x_ref[:, at].astype(f32) * inverse * gain).astype(bf16)
            if p < n_seq:
                kq_ref[p, which] = normed
            else:
                extra_ref[p - n_seq, 2 if which == 0 else 0] = normed
    for p in range(n_seq, heads):
        extra_ref[p - n_seq, 1] = do_ref[:, cols(order_ref[p])]
        extra_ref[p - n_seq, 3] = v_ref[:, cols(order_ref[p])]


def merge_kernel(n_seq, heads, order_ref, main_ref, extra_ref, out_ref, grad_v_ref):
    for p in range(heads):
        at = cols(order_ref[p])
        out_ref[:, at] = main_ref[p, 0] if p < n_seq else extra_ref[p - n_seq, 0]
        grad_v_ref[:, at] = main_ref[p, 1] if p < n_seq else extra_ref[p - n_seq, 3]


def back_kernel(n_seq, heads, order_ref, main_ref, extra_ref, q_ref, k_ref, gain_ref, gq_ref, gk_ref, ready, flush):
    ready(2)
    ready(1)
    scale = 1.0 / (heads * head_width)
    for which, x_ref, out_ref in ((0, q_ref, gq_ref), (1, k_ref, gk_ref)):
        ready(3 + which)

        def pieces(p):
            at = cols(order_ref[p])
            up = main_ref[p, pl.ds(which * tile_rows, tile_rows)] if p < n_seq else extra_ref[p - n_seq, 1 + which]
            gain = gain_ref[which : which + 1, at].astype(f32)
            return at, x_ref[:, at].astype(f32), gain * up.astype(f32)

        squares = jnp.zeros(block, f32)
        inner = jnp.zeros(block, f32)
        for p in range(heads):
            at, x, weighted = pieces(p)
            squares += x * x
            inner += weighted * x
        inverse = lax.rsqrt(jnp.sum(squares, axis=1, keepdims=True) * scale + norm_eps)
        pull = inverse * inverse * inverse * (jnp.sum(inner, axis=1, keepdims=True) * scale)
        inverse = jnp.broadcast_to(inverse, block)
        pull = jnp.broadcast_to(pull, block)
        for p in range(heads):
            at, x, weighted = pieces(p)
            out_ref[:, at] = (inverse * weighted - x * pull).astype(bf16)
        flush(which)


def fold_rows(values, combine):
    return combine(values.reshape(values.shape[0] // 8, 8, values.shape[1]), axis=0)


def attention_kernel(parts, most, n_query, n_tiles, group, at, *refs):
    names = ["table", *at["operands"], *at["results"], *at["scratch"]]
    r = dict(zip(names, refs))
    table = r["table"]
    stride = most + 1
    score_scale = log2e / math.sqrt(head_width)
    grad_scale = 1.0 / math.sqrt(head_width)
    key, value, query_of, grad_of = (
        functools.partial(at[k], r) for k in ("key", "value", "query", "grad")
    )
    forward, backward = "forward" in parts, "backward" in parts

    if "prologue" in at:
        at["prologue"](r)
    ahead = at["ahead"]

    @pl.loop(0, n_tiles // unrolled)
    def _(step):
        for t in [step * unrolled + u for u in range(unrolled)]:
            if forward:
                r["dv"][t] = jnp.zeros(block, f32)
            if backward:
                r["dk"][t] = jnp.zeros(block, f32)
            if forward and ahead:
                r["vt"][t] = value(t).T
            if backward and ahead:
                r["kt"][t] = key(t).T

    if backward:
        r["sums"][...] = jnp.zeros(r["sums"].shape, f32)

    def turned(name, t):
        if ahead:
            return r[name][t]
        return (value(t) if name == "vt" else key(t)).T

    def body(count, tiles, counts):
        for a, (i, n) in enumerate(zip(tiles, counts)):
            query, grad = query_of(i), grad_of(i)
            listed = [table[i * stride + j] for j in range(count)]

            def scores(j):
                s = dot(key(listed[j]), query, (1, 1)) * score_scale
                return jnp.where(j < n, s, masked_out) if j else s

            if forward:
                scratch = r["scores"]
                high = None
                for j in range(count):
                    s = scores(j)
                    scratch[a, j] = s
                    peak = fold_rows(s, jnp.max)
                    high = peak if high is None else jnp.maximum(high, peak)
                high = jnp.max(high, axis=0, keepdims=True)
                total = None
                for j in range(count):
                    p = jnp.exp2(scratch[a, j] - high)
                    scratch[a, j] = p
                    part = fold_rows(p, jnp.sum)
                    total = part if total is None else total + part
                total = jnp.sum(total, axis=0, keepdims=True)
                r["lse"][pl.ds(i, 1), :] = high * ln2 + jnp.log(total)
                inverse = 1.0 / total
                probs = [(scratch[a, j] * inverse).astype(bf16) for j in range(count)]
                values_t = jnp.concatenate([turned("vt", t) for t in listed], axis=1)
                out_t = dot(values_t, jnp.concatenate(probs, axis=0), (1, 0)).astype(bf16)
                at["store_out"](r, i, out_t.T)
                delta = jnp.sum(grad.T.astype(f32) * out_t.astype(f32), axis=0, keepdims=True)
                for j, t in enumerate(listed):
                    r["dv"][t] += dot(probs[j], grad, (1, 0))
                if not backward:
                    r["delta"][pl.ds(i, 1), :] = delta
            if backward:
                if not forward:
                    delta = r["delta"][pl.ds(i, 1), :]
                    lse = r["lse"][pl.ds(i, 1), :] * log2e
                if not forward:
                    for j in range(count):
                        r["scores"][a, j] = scores(j)
                for j, t in enumerate(listed):
                    r["dprobs"][a, j] = dot(value(t), grad, (1, 1))
                dscores = []
                for j in range(count):
                    s = r["scores"][a, j]
                    p = s * inverse if forward else jnp.exp2(s - lse)
                    dscores.append((p * (r["dprobs"][a, j] - delta)).astype(bf16))
                for j, t in enumerate(listed):
                    r["dk"][t] += dot(dscores[j], query, (1, 0))
                keys_t = jnp.concatenate([turned("kt", t) for t in listed], axis=1)
                dq_t = dot(keys_t, jnp.concatenate(dscores, axis=0), (1, 0)) * grad_scale
                dq = dq_t.astype(bf16).T
                at["store_dq"](r, i, dq)
                r["sums"][0] += fold_rows(dq.astype(f32) * query.astype(f32), jnp.sum)

    @pl.loop(0, n_query // group)
    def _(g):
        tiles = [g * group + a for a in range(group)]
        counts = [table[t * stride + most] for t in tiles]
        top = functools.reduce(jnp.maximum, counts)
        for static_count in range(1, most + 1):

            @pl.when(top == static_count)
            def _():
                body(static_count, tiles, counts)

    def store_grads(t, where):
        if forward:
            at["store_dv"](r, where, r["dv"][t].astype(bf16))
        if backward:
            dk = (r["dk"][t] * grad_scale).astype(bf16)
            at["store_dk"](r, where, dk)
            r["sums"][1] += fold_rows(dk.astype(f32) * key(t).astype(f32), jnp.sum)

    at["epilogue"](r, store_grads)

    if backward:
        for m in range(2):
            r["gains"][m : m + 1, :] = jnp.sum(r["sums"][m], axis=0, keepdims=True)


def setter(name, where):
    def store(r, i, values):
        r[name][where(i)] = values

    return store


def store_dk_first(r, t, values):
    r["dqk"][t, pl.ds(tile_rows, tile_rows)] = values
    r["dqk"][t, pl.ds(2 * tile_rows, shared_rows)] = jnp.zeros((shared_rows, head_width), bf16)


def every_tile(n_tiles, r, store):
    @pl.loop(0, n_tiles // unrolled)
    def _(step):
        for u in range(unrolled):
            store(step * unrolled + u, step * unrolled + u)


def load_shifted(n_x, n_z, r):
    x_index = r["table"][r["table"].shape[0] - 1]
    for s in range(n_x):
        x = lax.rem(x_index + n_x - s, n_x)
        for z in range(n_z):
            name, at = ("own" if s == 0 else f"kv{s}"), z
            if s == 2 and z >= n_z // 2:
                name, at = "kv2_rest", z - n_z // 2
            for m in range(2):
                r["kv"][z * n_x + x, m] = r[name][at, m + 2 if s == 0 else m]


def store_shifted(n_x, n_z, r, store):
    x_index = r["table"][r["table"].shape[0] - 1]
    for s in range(n_x):
        x = lax.rem(x_index + s, n_x)

        @pl.loop(0, n_z)
        def _(z):
            store(z * n_x + x, (s, z))


def store_part(m):
    def store(r, where, values):
        s, z = where
        r[f"part{s}"][z, m] = values

    return store


def add_kernel(one_ref, two_ref, sum_ref):
    @pl.loop(0, sum_ref.shape[0])
    def _(z):
        sum_ref[z] = (one_ref[z].astype(f32) + two_ref[z].astype(f32)).astype(bf16)


def collect_kernel(odq_ref, *refs):
    parts, back_ref = refs[:-1], refs[-1]

    @pl.loop(0, back_ref.shape[0])
    def _(z):
        for m in range(2):
            back_ref[z, m] = odq_ref[z, m]
            total = sum(part[z, m].astype(f32) for part in parts)
            back_ref[z, 2 + m] = total.astype(bf16)


shared_rows = 32


def share_kernel(sums_ref, lse_ref, unused_hbm, back_hbm, terms_ref, rows_ref, sems):
    value = sums_ref[...]
    for term in range(2):
        part = value.astype(bf16).astype(f32)
        terms_ref[4 * term : 4 * term + 4, :] = part
        value = value - part
    value = lse_ref[...]
    for term in range(1, 4):
        part = value.astype(bf16).astype(f32)
        terms_ref[8 * term : 8 * term + 8, :] = part
        value = value - part
    rows_ref[...] = terms_ref[...].astype(bf16)
    n_seq, n_rows = back_hbm.shape[:2]
    last = pl.ds(n_rows - shared_rows, shared_rows)
    copies = [pltpu.make_async_copy(rows_ref, back_hbm.at[d, last], sems.at[d]) for d in range(n_seq)]
    for copy in copies:
        copy.start()
    for copy in copies:
        copy.wait()


def finish_kernel(n_x, n_z, heads, per, order_ref, slot_ref, here_ref, lse_ref, gq_ref, gk_ref, home_hbm, out_ref, sq_ref, sk_ref, rows_ref, shared_ref, held_ref, sem):
    n_seq = n_x * n_z
    own, f_index = here_ref[0], here_ref[1]
    last = pl.ds(home_hbm.shape[1] - shared_rows, shared_rows)
    copy = pltpu.make_async_copy(home_hbm.at[:, last], rows_ref, sem)
    copy.start()
    copy.wait()
    shared_ref[...] = rows_ref[...].astype(f32)

    def row(device, line):
        lines = [8 * t + line for t in range(1, 4)] if line < n_z else [line - n_z, line - n_z + 4]
        return sum(shared_ref[device, n : n + 1, :] for n in lines)

    held_ref[...] = jnp.zeros(held_ref.shape, f32)
    held_ref[lax.rem(slot_ref[order_ref[own]], 2)] = lse_ref[...]

    @pl.loop(0, heads - n_seq)
    def _(e):
        slot = slot_ref[order_ref[n_seq + e]]

        @pl.when(lax.div(slot, 2) == own)
        def _():
            for x in range(n_x):
                for z in range(n_z):
                    at = z * n_x + x
                    held_ref[lax.rem(slot, 2), at : at + 1, :] = row(e * n_x + x, z)

    for s in range(2):
        for t in range(n_seq):
            out_ref[s : s + 1, cols(t)] = held_ref[s, t : t + 1, :]

    factor = 1.0 / math.sqrt(n_seq * tile_rows * (heads // per))
    for j in range(per):
        position = order_ref[heads + f_index * per + j]
        for m, (gain_ref, out) in enumerate(((gq_ref, sq_ref), (gk_ref, sk_ref))):
            first = row(jnp.minimum(position, n_seq - 1), n_z + m)
            spread = jnp.maximum(position - n_seq, 0) * n_x
            second = sum(row(spread + x, n_z + 2 + m) for x in range(n_x))
            total = jnp.where(position < n_seq, first, second)
            out[j : j + 1, :] = total / gain_ref[j : j + 1, :].astype(f32) * factor


def after(values, done):
    return lax.optimization_barrier((values, done))[0]


def shards(query_in, key_in, value_in, out_grad, gain_q, gain_k, mask_lists, tile_counts, head_slot):
    n_x, n_z, n_f = lax.axis_size("x"), lax.axis_size("z"), lax.axis_size("fsdp")
    n_seq = n_x * n_z
    x_index, z_index, f_index = lax.axis_index("x"), lax.axis_index("z"), lax.axis_index("fsdp")
    own = z_index * n_x + x_index
    heads, n_tiles, most = mask_lists.shape
    extra = heads - n_seq
    features = heads * head_width
    seq_axes = ("z", "x")
    q2, k2, v2, g2 = (a.reshape(tile_rows, features) for a in (query_in, key_in, value_in, out_grad))

    def swap(values, axes):
        return lax.all_to_all(values, axes, split_axis=0, concat_axis=0, tiled=True)

    order, value_send = pl.pallas_call(
        functools.partial(place_kernel, n_seq, heads),
        out_shape=(
            jax.ShapeDtypeStruct((2 * heads,), i32),
            jax.ShapeDtypeStruct((n_seq, *block), bf16),
        ),
        in_specs=[smem, hbm],
        out_specs=(smem, hbm),
        scratch_shapes=[
            pltpu.SMEM((2 * n_seq,), i32),
            pltpu.VMEM((tile_rows, features), bf16),
            pltpu.SemaphoreType.DMA,
            pltpu.SemaphoreType.DMA((n_seq,)),
        ],
        compiler_params=pltpu.CompilerParams(vmem_limit_bytes=most_vmem),
        name="place_heads",
    )(head_slot, v2)
    value_main = swap(value_send, seq_axes)

    gains = lax.all_gather(jnp.stack([gain_q, gain_k]), "fsdp", axis=1, tiled=True)
    kq_send, grad_send, extra_send = call(
        functools.partial(norm_kernel, n_seq, heads),
        "normalize",
        [((n_seq, 2, *block), bf16), ((n_seq, *block), bf16), ((extra, 4, *block), bf16)],
        [smem] + [vmem] * 5,
        7 * heads,
        hbm_in=(1, 2, 3, 4),
        hbm_out=(0, 1, 2),
    )(order, q2, k2, v2, g2, gains)
    table = jnp.concatenate([mask_lists, tile_counts[:, :, None]], axis=2)
    table_main = lax.dynamic_index_in_dim(table, order[own], 0, keepdims=False).reshape(-1)
    table_extra = lax.dynamic_index_in_dim(table, order[n_seq + z_index], 0, keepdims=False)
    table_extra = lax.dynamic_index_in_dim(
        table_extra.reshape(n_z, n_x, most + 1), x_index, 1, keepdims=False
    )
    table_extra = jnp.concatenate([table_extra.reshape(-1), x_index[None]])
    extra_own = swap(after(extra_send, (value_main, table_main, table_extra)), "z")

    def attention(parts, name, n_query, at, outs, n_operands, passes, hbm_in=(), hbm_out=()):
        group = 2
        tile_f32 = pltpu.VMEM((n_tiles, *block), f32)
        tile_bf16 = pltpu.VMEM((n_tiles, *block), bf16)
        scratch = {"scores": pltpu.VMEM((group, most, *block), f32)}
        if "forward" in parts:
            scratch |= {"vt": tile_bf16, "dv": tile_f32}
        if "backward" in parts:
            scratch |= {"kt": tile_bf16, "dk": tile_f32, "sums": pltpu.VMEM((2, 8, head_width), f32)}
            scratch["dprobs"] = scratch["scores"]
        if not at["ahead"]:
            scratch = {n: v for n, v in scratch.items() if n not in ("kt", "vt")}
            scratch["kv"] = pltpu.VMEM((n_tiles, 2, *block), bf16)
        at = {**at, "scratch": list(scratch), "results": list(outs)}
        return call(
            functools.partial(attention_kernel, parts, most, n_query, n_tiles, group, at),
            name,
            list(outs.values()),
            [smem] + [vmem] * n_operands,
            10 * n_tiles,
            flops=n_query * most * passes * 2 * tile_rows * tile_rows * head_width,
            scratch=list(scratch.values()),
            hbm_in=hbm_in,
            hbm_out=hbm_out,
        )

    rows_of = lambda n: ((n, tile_rows), f32)

    def shift(values, s):
        return lax.ppermute(values, "x", [(x, (x + s) % n_x) for x in range(n_x)])

    kv_own = extra_own[:, 2:4]
    kv_left, kv_right = shift(kv_own, 1), shift(kv_own, n_x - 1)
    half = n_z // 2
    kv_shifted = [kv_left, shift(kv_left[:half], 1), shift(kv_right[half:], n_x - 1), kv_right]
    grad_main = swap(after(grad_send, extra_own), seq_axes)
    kq_main = swap(after(kq_send, (grad_main, kv_shifted)), seq_axes)
    kv_shifted = after(kv_shifted, grad_main)
    odq_extra, lse_extra, gain_extra, *dkv_parts = attention(
        ("forward", "backward"),
        "attention_second",
        n_z,
        {
            "operands": ["own", "kv1", "kv2", "kv2_rest", "kv3"],
            "key": lambda r, t: r["kv"][t, 0],
            "value": lambda r, t: r["kv"][t, 1],
            "query": lambda r, i: r["own"][i, 0],
            "grad": lambda r, i: r["own"][i, 1],
            "ahead": False,
            "prologue": functools.partial(load_shifted, n_x, n_z),
            "epilogue": functools.partial(store_shifted, n_x, n_z),
            "store_out": setter("odq", lambda i: (i, 0)),
            "store_dq": setter("odq", lambda i: (i, 1)),
            "store_dk": store_part(0),
            "store_dv": store_part(1),
        },
        {
            "odq": ((n_z, 2, *block), bf16),
            "lse": rows_of(n_z),
            "gains": ((2, head_width), f32),
            **{f"part{s}": ((n_z, 2, *block), bf16) for s in range(n_x)},
        },
        n_x + 1,
        20,
    )(table_extra, extra_own, *kv_shifted)
    relayed = shift(dkv_parts[2], n_x - 1)
    (joined,) = call(add_kernel, "add_parts", [((n_z, 2, *block), bf16)], [vmem] * 2, 6 * n_z)(
        dkv_parts[3], relayed
    )
    dkv_parts = [dkv_parts[0], shift(dkv_parts[1], 1), shift(joined, n_x - 1)]
    main_at = {
        "ahead": True,
        "epilogue": functools.partial(every_tile, n_tiles),
        "key": lambda r, t: r["kq"][t, 0],
        "value": lambda r, t: r["v"][t],
        "query": lambda r, i: r["kq"][i, 1],
        "grad": lambda r, i: r["g"][i],
    }
    (extra_back,) = call(
        collect_kernel, "collect", [((n_z, 4, *block), bf16)], [vmem] * 4, 12 * n_z
    )(odq_extra, *dkv_parts)
    extra_home = swap(after(extra_back, kq_main), "z")
    odv_main, lse_main, delta_main = attention(
        ("forward",),
        "forward_first",
        n_tiles,
        {
            **main_at,
            "operands": ["kq", "v", "g"],
            "store_out": setter("odv", lambda i: (i, 0)),
            "store_dv": setter("odv", lambda t: (t, 1)),
        },
        {"odv": ((n_tiles, 2, *block), bf16), "lse": rows_of(n_tiles), "delta": rows_of(n_tiles)},
        3,
        10,
        hbm_in=(1, 2, 3),
        hbm_out=(0,),
    )(table_main, kq_main, value_main, grad_main)
    odv_home = swap(after(odv_main, extra_home), seq_axes)
    dqk_main, gain_main = attention(
        ("backward",),
        "backward_first",
        n_tiles,
        {
            **main_at,
            "operands": ["kq", "v", "g", "lse", "delta"],
            "store_dq": setter("dqk", lambda i: (i, pl.ds(0, tile_rows))),
            "store_dk": store_dk_first,
        },
        {"dqk": ((n_tiles, 2 * tile_rows + shared_rows, head_width), bf16), "gains": ((2, head_width), f32)},
        5,
        16,
        hbm_in=(1, 2, 3),
        hbm_out=(0,),
    )(table_main, kq_main, value_main, grad_main, lse_main, delta_main)

    gain_sums = lax.psum(jnp.concatenate([gain_main, gain_extra]), "fsdp")
    dqk_shape = (n_tiles, 2 * tile_rows + shared_rows, head_width)
    dqk_main = pl.pallas_call(
        share_kernel,
        out_shape=jax.ShapeDtypeStruct(dqk_shape, bf16),
        in_specs=[vmem, vmem, hbm],
        out_specs=hbm,
        input_output_aliases={2: 0},
        scratch_shapes=[
            pltpu.VMEM((shared_rows, head_width), f32),
            pltpu.VMEM((shared_rows, head_width), bf16),
            pltpu.SemaphoreType.DMA((n_seq,)),
        ],
        compiler_params=pltpu.CompilerParams(vmem_limit_bytes=most_vmem),
        name="share_rows",
    )(gain_sums, lse_extra, dqk_main)
    dqk_home = swap(after(dqk_main, odv_home), seq_axes)

    wide = ((tile_rows, features), bf16)
    attn_out, grad_v = call(
        functools.partial(merge_kernel, n_seq, heads),
        "merge_heads",
        [wide, wide],
        [smem, vmem, vmem],
        4 * heads,
        hbm_in=(1, 2),
        hbm_out=(0, 1),
    )(order, odv_home, extra_home)
    grad_q, grad_k = call(
        functools.partial(back_kernel, n_seq, heads),
        "gradients_home",
        [wide, wide],
        [smem] + [vmem] * 5,
        6 * heads,
        hbm_in=(2, 1, 3, 4),
        hbm_out=(0, 1),
        lazy=True,
    )(order, dqk_home, extra_home, q2, k2, gains)

    per = heads // n_f
    lse_slots, share_q, share_k = call(
        functools.partial(finish_kernel, n_x, n_z, heads, per),
        "finish",
        [((2, n_tiles * tile_rows), f32), ((per, head_width), f32), ((per, head_width), f32)],
        [smem] * 3 + [vmem] * 3 + [hbm],
        32,
        scratch=[
            pltpu.VMEM((n_seq, shared_rows, head_width), bf16),
            pltpu.VMEM((n_seq, shared_rows, head_width), f32),
            pltpu.VMEM((2, n_tiles, tile_rows), f32),
            pltpu.SemaphoreType.DMA,
        ],
        room=most_vmem,
    )(
        order,
        head_slot,
        jnp.stack([own, f_index]),
        lse_main,
        gain_q.reshape(per, head_width),
        gain_k.reshape(per, head_width),
        dqk_home,
    )
    whole = lambda a: a.reshape(1, tile_rows, features)
    return (
        whole(attn_out),
        lse_slots[None],
        whole(grad_q),
        whole(grad_k),
        whole(grad_v),
        share_q.reshape(-1),
        share_k.reshape(-1),
    )


def solution(mesh):
    n_seq, n_f = mesh.devices.shape
    n_z = 8
    grid = Mesh(mesh.devices.reshape(n_z, n_seq // n_z, n_f), ("z", "x", "fsdp"))
    rows = P("fsdp", ("z", "x"), None)
    in_specs = (rows,) * 4 + (P("fsdp"),) * 2 + (P(),) * 3
    out_specs = (rows,) * 5 + (P("fsdp"),) * 2
    return jax.shard_map(shards, mesh=grid, in_specs=in_specs, out_specs=out_specs, check_vma=False)
```

profile of v0, /device:TPU:4, one launch (start us, length us, event | category | flops | bytes accessed | tf_op | source)
XLA Modules:
  0.0 347.1 jit_solution(5351555893908702499)
XLA Ops:
  0.6 3.7 %place_heads.1 = (s32[80]{0:T(128)}, bf16[32,128,128]{2,1,0:T(8,128)(2,1)}) custom-call(s32[40]{0:T(128)} %slot_ref.3, bf16[128,5120]{1,0:T(8,128)(2,1)} %bitcast.20), custom_call_target="tpu_custom_call" | custom-call | tf_op jit(solution)/shard_map/place_heads/pallas_call | solution.py:468
  4.4 11.7 %all-to-all-start = ((bf16[32,128,128]{2,1,0:T(8,128)(2,1)}), bf16[32,128,128]{2,1,0:T(8,128)(2,1)S(1)}, u32[]{:S(2)}, u32[]{:S(2)}) async-start(bf16[32,128,128]{2,1,0:T(8,128)(2,1)} %get-tuple-element.45), calls=%async_computation | async-start | bytes 2097152 | tf_op jit(solution)/shard_map/all_to_all | solution.py:466
  22.3 13.8 %all_gather.3.refs_5_ = bf16[2,5120]{1,0:T(2,128)(2,1)} all-gather(bf16[2,640]{1,0:T(2,128)(2,1)S(1)} %pad_maximum_fusion), channel_id=1, replica_groups=mesh['z'=8,'x'=4,'fsdp'=8] {'fsdp'}, dimensions={1}, use_global_device_ids=true | all-gather | bytes 23040 | tf_op jit(solution)/shard_map/all_gather | solution.py:487
  36.1 6.7 %normalize.1 = (bf16[32,2,128,128]{3,2,1,0:T(8,128)(2,1)}, bf16[32,128,128]{2,1,0:T(8,128)(2,1)}, bf16[8,4,128,128]{3,2,1,0:T(8,128)(2,1)}) custom-call(s32[80]{0:T(128)} %get-tuple-element.41.refs_0_.order_ref, bf16[128,5120]{1,0:T(8,128)(2,1)} %bitcast.22, bf16[128,5120]{1,0:T(8,128)(2,1)} %bitcast.24, bf16[128,5120]{1,0:T(8,128)(2,1)} %bitcast.21, ...), custom_call_target="tpu_custom_call" | custom-call | bytes 9175040 | tf_op jit(solution)/shard_map/normalize/pallas_call | solution.py:71
  42.9 1.3 all-to-all-done.refs_2_
  45.2 34.6 %all_to_all.35.refs_1_ = bf16[8,4,128,128]{3,2,1,0:T(8,128)(2,1)S(1)} all-to-all(bf16[8,4,128,128]{3,2,1,0:T(8,128)(2,1)} %get-tuple-element.46), channel_id=1, replica_groups=mesh['z'=8,'x'=4,'fsdp'=8] {'z'}, dimensions={0} | all-to-all | bytes 2097152 | tf_op jit(solution)/shard_map/all_to_all | solution.py:466
  79.8 5.0 %all-to-all-start.2 = ((bf16[32,128,128]{2,1,0:T(8,128)(2,1)}), bf16[32,128,128]{2,1,0:T(8,128)(2,1)}, u32[]{:S(2)}, u32[]{:S(2)}) async-start(bf16[32,128,128]{2,1,0:T(8,128)(2,1)} %get-tuple-element.47), calls=%async_computation.2 | async-start | bytes 2097152 | tf_op jit(solution)/shard_map/all_to_all | solution.py:466
  85.5 1.5 collective-permute-start
  86.9 21.8 %collective-permute-done.2.refs_5_ = bf16[8,2,128,128]{3,2,1,0:T(8,128)(2,1)S(1)} collective-permute-done((bf16[8,2,128,128]{3,2,1,0:T(8,128)(2,1)S(1)}, bf16[8,2,128,128]{3,2,1,0:T(8,128)(2,1)S(1)}, u32[]{:S(2)}, u32[]{:S(2)}) %collective-permute-start.2) | collective-permute-done | bytes 524320 | tf_op jit(solution)/shard_map/ppermute | solution.py:535
  109.0 2.0 collective-permute-start.1
  111.0 5.7 %collective-permute-done.3.refs_4_ = bf16[4,2,128,128]{3,2,1,0:T(8,128)(2,1)S(1)} collective-permute-done((bf16[4,2,128,128]{3,2,1,0:T(8,128)(2,1)S(1)}, bf16[4,2,128,128]{3,2,1,0:T(8,128)(2,1)S(1)}, u32[]{:S(2)}, u32[]{:S(2)}) %collective-permute-start.3) | collective-permute-done | bytes 262176 | tf_op jit(solution)/shard_map/ppermute | solution.py:535
  116.7 11.2 %all-to-all-start.3 = ((bf16[32,2,128,128]{3,2,1,0:T(8,128)(2,1)}), bf16[32,2,128,128]{3,2,1,0:T(8,128)(2,1)}, u32[]{:S(2)}, u32[]{:S(2)}) async-start(bf16[32,2,128,128]{3,2,1,0:T(8,128)(2,1)} %get-tuple-element.48), calls=%async_computation.3 | async-start | bytes 4194304 | tf_op jit(solution)/shard_map/all_to_all | solution.py:466
  127.9 10.3 %attention_second.1 = (bf16[8,2,128,128]{3,2,1,0:T(8,128)(2,1)S(1)}, f32[8,128]{1,0:T(8,128)S(1)}, f32[2,128]{1,0:T(2,128)S(1)}, bf16[8,2,128,128]{3,2,1,0:T(8,1...) custom-call(s32[97]{0:T(128)S(1)} %pad_add_fusion.refs_0_, ...), custom_call_target="tpu_custom_call" | custom-call | flops 7381975040 | bytes 10485760 | tf_op jit(solution)/shard_map/attention_second/pallas_call | solution.py:71
  138.8 1.5 collective-permute-start.4
  140.3 19.2 %collective-permute-done.5.two_ref = bf16[8,2,128,128]{3,2,1,0:T(8,128)(2,1)S(1)} collective-permute-done((bf16[8,2,128,128]{3,2,1,0:T(8,128)(2,1)S(1)}, bf16[8,2,128,128]{3,2,1,0:T(8,128)(2,1)S(1)}, u32[]{:S(2)}, u32[]{:S(2)}) %collective-permute-start.5) | collective-permute-done | bytes 524320 | tf_op jit(solution)/shard_map/ppermute | solution.py:535
  159.7 1.8 collective-permute-start.6
  161.4 15.8 %collective-permute-done.6.refs_2_ = bf16[8,2,128,128]{3,2,1,0:T(8,128)(2,1)S(1)} collective-permute-done((bf16[8,2,128,128]{3,2,1,0:T(8,128)(2,1)S(1)}, bf16[8,2,128,128]{3,2,1,0:T(8,128)(2,1)S(1)}, u32[]{:S(2)}, u32[]{:S(2)}) %collective-permute-start.6) | collective-permute-done | bytes 524320 | tf_op jit(solution)/shard_map/ppermute | solution.py:535
  177.2 1.2 collect.1
  178.5 6.8 %all-to-all-start.4 = ((bf16[8,4,128,128]{3,2,1,0:T(8,128)(2,1)}), bf16[8,4,128,128]{3,2,1,0:T(8,128)(2,1)S(1)}, u32[]{:S(2)}, u32[]{:S(2)}) async-start(bf16[8,4,128,128]{3,2,1,0:T(8,128)(2,1)} %collect.1), calls=%async_computation.4 | async-start | bytes 2097152 | tf_op jit(solution)/shard_map/all_to_all | solution.py:466
  185.2 26.9 %forward_first.1 = (bf16[32,2,128,128]{3,2,1,0:T(8,128)(2,1)}, f32[32,128]{1,0:T(8,128)}, f32[32,128]{1,0:T(8,128)}) custom-call(s32[384]{0:T(512)} %reshape.63.refs_0_, bf16[32,2,128,128]{3,2,1,0:T(8,128)(2,1)} %all-to-all-done.3.refs_1_, bf16[32,128,128]{2,1,0:T(8,128)(2,1)} %copy-done.4, bf16[32,128,128]{2,1,0:T(8,128)(2,1)} %all-to-all-done.2.refs_3_), custom_call_target="tpu_custom_call" | custom-call | flops 14763950080 | bytes 10485760 | tf_op jit(solution)/shard_map/forward_first/pallas_call | solution.py:71
  214.1 10.2 %all-to-all-start.5 = ((bf16[32,2,128,128]{3,2,1,0:T(8,128)(2,1)}), bf16[32,2,128,128]{3,2,1,0:T(8,128)(2,1)S(1)}, u32[]{:S(2)}, u32[]{:S(2)}) async-start(bf16[32,2,128,128]{3,2,1,0:T(8,128)(2,1)} %get-tuple-element.60), calls=%async_computation.5 | async-start | bytes 4194304 | tf_op jit(solution)/shard_map/all_to_all | solution.py:466
  224.4 27.9 %backward_first.1 = (bf16[32,288,128]{2,1,0:T(8,128)(2,1)}, f32[2,128]{1,0:T(2,128)}) custom-call(s32[384]{0:T(512)} %reshape.63.refs_0_, bf16[32,2,128,128]{3,2,1,0:T(8,128)(2,1)} %all-to-all-done.3.refs_1_, bf16[32,128,128]{2,1,0:T(8,128)(2,1)} %copy-done.4, bf16[32,128,128]{2,1,0:T(8,128)(2,1)} %all-to-all-done.2.refs_3_, ...), custom_call_target="tpu_custom_call" | custom-call | flops 23622320128 | bytes 10485760 | tf_op jit(solution)/shard_map/backward_first/pallas_call | solution.py:71
  253.0 13.3 %psum.7.sums_ref = f32[4,128]{1,0:T(4,128)} all-reduce(f32[4,128]{1,0:T(4,128)S(1)} %pad_maximum_fusion.1), channel_id=1, replica_groups=mesh['z'=8,'x'=4,'fsdp'=8] {'fsdp'}, use_global_device_ids=true, to_apply=%region_0.1 | all-reduce | flops 512 | bytes 4096 | tf_op jit(solution)/shard_map/psum | solution.py:622
  266.3 1.8 share_rows.1
  268.0 4.8 %all-to-all-done.5.refs_1_ = bf16[32,2,128,128]{3,2,1,0:T(8,128)(2,1)S(1)} async-done(((bf16[32,2,128,128]{3,2,1,0:T(8,128)(2,1)}), bf16[32,2,128,128]{3,2,1,0:T(8,128)(2,1)S(1)}, u32[]{:S(2)}, u32[]{:S(2)}) %all-to-all-start.5) | async-done | bytes 2097184 | tf_op jit(solution)/shard_map/all_to_all | solution.py:466
  272.8 1.3 copy-done.3
  274.1 6.5 %all-to-all-start.6 = ((bf16[32,288,128]{2,1,0:T(8,128)(2,1)}), bf16[32,288,128]{2,1,0:T(8,128)(2,1)S(1)}, u32[]{:S(2)}, u32[]{:S(2)}) async-start(bf16[32,288,128]{2,1,0:T(8,128)(2,1)} %share_rows.1), calls=%async_computation.6 | async-start | bytes 4718592 | tf_op jit(solution)/shard_map/all_to_all | solution.py:466
  281.3 4.8 %merge_heads.1 = (bf16[128,5120]{1,0:T(8,128)(2,1)}, bf16[128,5120]{1,0:T(8,128)(2,1)}) custom-call(s32[80]{0:T(128)} %get-tuple-element.41.refs_0_.order_ref, bf16[32,2,128,128]{3,2,1,0:T(8,128)(2,1)} %copy-done.3, bf16[8,4,128,128]{3,2,1,0:T(8,128)(2,1)} %copy-done.2), custom_call_target="tpu_custom_call" | custom-call | bytes 5242880 | tf_op jit(solution)/shard_map/merge_heads/pallas_call | solution.py:71
  286.1 49.6 %all-to-all-done.6.home_hbm.refs_1_ = bf16[32,288,128]{2,1,0:T(8,128)(2,1)S(1)} async-done(((bf16[32,288,128]{2,1,0:T(8,128)(2,1)}), bf16[32,288,128]{2,1,0:T(8,128)(2,1)S(1)}, u32[]{:S(2)}, u32[]{:S(2)}) %all-to-all-start.6) | async-done | bytes 2359328 | tf_op jit(solution)/shard_map/all_to_all | solution.py:466
  335.7 1.4 copy-done.1
  337.1 7.1 %gradients_home.1 = (bf16[128,5120]{1,0:T(8,128)(2,1)}, bf16[128,5120]{1,0:T(8,128)(2,1)}) custom-call(s32[80]{0:T(128)} %get-tuple-element.41.refs_0_.order_ref, bf16[32,288,128]{2,1,0:T(8,128)(2,1)} %copy-done.1, bf16[8,4,128,128]{3,2,1,0:T(8,128)(2,1)} %copy-done.2, bf16[128,5120]{1,0:T(8,128)(2,1)} %bitcast.23, bf16[128,5120]{1,0:T(8,128)(2,1)} %bitcast.25, ...), custom_call_target="tpu_custom_call" | custom-call | bytes 7864320 | tf_op jit(solution)/shard_map/gradients_home/pallas_call | solution.py:71
  344.2 2.6 finish.1
  (44 shorter events, 8.3 us)
Async XLA Ops:
  4.4 11.8 %copy-start.6 = (s32[80]{0:T(128)S(1)}, s32[80]{0:T(128)}, u32[]{:S(2)}) copy-start(s32[80]{0:T(128)} %get-tuple-element.41.refs_0_.order_ref) | copy-start | bytes 964
  4.4 15.0 %copy-start.9 = (bf16[640]{0:T(1024)(128)(2,1)S(1)}, bf16[640]{0:T(1024)(128)(2,1)}, u32[]{:S(2)}) copy-start(bf16[640]{0:T(1024)(128)(2,1)} %param.13) | copy-start | bytes 3844
  4.4 15.0 %copy-start.8 = (bf16[640]{0:T(1024)(128)(2,1)S(1)}, bf16[640]{0:T(1024)(128)(2,1)}, u32[]{:S(2)}) copy-start(bf16[640]{0:T(1024)(128)(2,1)} %param.14) | copy-start | bytes 3844
  4.4 16.3 %copy-start.5 = (s32[40,32,11]{0,1,2:T(8,128)S(1)}, s32[40,32,11]{0,1,2:T(8,128)}, u32[]{:S(2)}) copy-start(s32[40,32,11]{0,1,2:T(8,128)} %param.15) | copy-start | bytes 168964
  4.4 16.3 %copy-start.7 = (s32[40,32]{0,1:T(8,128)S(1)}, s32[40,32]{0,1:T(8,128)}, u32[]{:S(2)}) copy-start(s32[40,32]{0,1:T(8,128)} %param.16) | copy-start | bytes 15364
  4.4 39.8 %all-to-all-start = ((bf16[32,128,128]{2,1,0:T(8,128)(2,1)}), bf16[32,128,128]{2,1,0:T(8,128)(2,1)S(1)}, u32[]{:S(2)}, u32[]{:S(2)}) async-start(bf16[32,128,128]{2,1,0:T(8,128)(2,1)} %get-tuple-element.45), calls=%async_computation | async-start | bytes 2097152 | tf_op jit(solution)/shard_map/all_to_all | solution.py:466
  44.2 1.0 copy-start.4
  79.8 36.9 %all-to-all-start.2 = ((bf16[32,128,128]{2,1,0:T(8,128)(2,1)}), bf16[32,128,128]{2,1,0:T(8,128)(2,1)}, u32[]{:S(2)}, u32[]{:S(2)}) async-start(bf16[32,128,128]{2,1,0:T(8,128)(2,1)} %get-tuple-element.47), calls=%async_computation.2 | async-start | bytes 2097152 | tf_op jit(solution)/shard_map/all_to_all | solution.py:466
  84.8 23.9 %collective-permute-start.2 = (bf16[8,2,128,128]{3,2,1,0:T(8,128)(2,1)S(1)}, bf16[8,2,128,128]{3,2,1,0:T(8,128)(2,1)S(1)}, u32[]{:S(2)}, u32[]{:S(2)}) collective-permute-start(bf16[8,2,128,128]{3,2,1,0:T(8,128)(2,1)S(1)} %slice.12), channel_id=1, source_target_pairs={{0,24},{8,0},{16,8},{24,16},{1,25},{9,1},{17,9},{25,17},{2,26},{10... | collective-permute-start | bytes 1572872 | tf_op jit(solution)/shard_map/ppermute | solution.py:535
  85.5 23.5 %collective-permute-start = (bf16[8,2,128,128]{3,2,1,0:T(8,128)(2,1)S(1)}, bf16[8,2,128,128]{3,2,1,0:T(8,128)(2,1)S(1)}, u32[]{:S(2)}, u32[]{:S(2)}) collective-permute-start(bf16[8,2,128,128]{3,2,1,0:T(8,128)(2,1)S(1)} %slice.12), channel_id=1, source_target_pairs={{0,8},{8,16},{16,24},{24,0},{1,9},{9,17},{17,25},{25,1},{2,10},{10... | collective-permute-start | bytes 1572872 | tf_op jit(solution)/shard_map/ppermute | solution.py:535
  108.8 7.9 %collective-permute-start.3 = (bf16[4,2,128,128]{3,2,1,0:T(8,128)(2,1)S(1)}, bf16[4,2,128,128]{3,2,1,0:T(8,128)(2,1)S(1)}, u32[]{:S(2)}, u32[]{:S(2)}) collective-permute-start(bf16[4,2,128,128]{3,2,1,0:T(8,128)(2,1)S(1)} %slice.14), channel_id=1, source_target_pairs={{0,24},{8,0},{16,8},{24,16},{1,25},{9,1},{17,9},{25,17},{2,26},{10... | collective-permute-start | bytes 786440 | tf_op jit(solution)/shard_map/ppermute | solution.py:535
  109.0 7.7 %collective-permute-start.1 = (bf16[4,2,128,128]{3,2,1,0:T(8,128)(2,1)S(1)}, bf16[4,2,128,128]{3,2,1,0:T(8,128)(2,1)S(1)}, u32[]{:S(2)}, u32[]{:S(2)}) collective-permute-start(bf16[4,2,128,128]{3,2,1,0:T(8,128)(2,1)S(1)} %slice.13), channel_id=1, source_target_pairs={{0,8},{8,16},{16,24},{24,0},{1,9},{9,17},{17,25},{25,1},{2,10},{10... | collective-permute-start | bytes 786440 | tf_op jit(solution)/shard_map/ppermute | solution.py:535
  116.7 61.8 %all-to-all-start.3 = ((bf16[32,2,128,128]{3,2,1,0:T(8,128)(2,1)}), bf16[32,2,128,128]{3,2,1,0:T(8,128)(2,1)}, u32[]{:S(2)}, u32[]{:S(2)}) async-start(bf16[32,2,128,128]{3,2,1,0:T(8,128)(2,1)} %get-tuple-element.48), calls=%async_computation.3 | async-start | bytes 4194304 | tf_op jit(solution)/shard_map/all_to_all | solution.py:466
  138.2 39.1 %copy-start = (f32[8,128]{1,0:T(8,128)}, f32[8,128]{1,0:T(8,128)S(1)}, u32[]{:S(2)}) copy-start(f32[8,128]{1,0:T(8,128)S(1)} %get-tuple-element.66.lse_ref) | copy-start | bytes 12292
  138.2 21.3 %collective-permute-start.5 = (bf16[8,2,128,128]{3,2,1,0:T(8,128)(2,1)S(1)}, bf16[8,2,128,128]{3,2,1,0:T(8,128)(2,1)S(1)}, u32[]{:S(2)}, u32[]{:S(2)}) collective-permute-start(bf16[8,2,128,128]{3,2,1,0:T(8,128)(2,1)S(1)} %get-tuple-element.58), channel_id=1, source_target_pairs={{0,24},{8,0},{16,8},{24,16},{1,25},{9,1},{17,9},{25,17},{2,26},{10... | collective-permute-start | bytes 1572872 | tf_op jit(solution)/shard_map/ppermute | solution.py:535
  138.8 22.6 %collective-permute-start.4 = (bf16[8,2,128,128]{3,2,1,0:T(8,128)(2,1)S(1)}, bf16[8,2,128,128]{3,2,1,0:T(8,128)(2,1)S(1)}, u32[]{:S(2)}, u32[]{:S(2)}) collective-permute-start(bf16[8,2,128,128]{3,2,1,0:T(8,128)(2,1)S(1)} %get-tuple-element.56), channel_id=1, source_target_pairs={{0,8},{8,16},{16,24},{24,0},{1,9},{9,17},{17,25},{25,1},{2,10},{10... | collective-permute-start | bytes 1572872 | tf_op jit(solution)/shard_map/ppermute | solution.py:535
  159.7 17.6 %collective-permute-start.6 = (bf16[8,2,128,128]{3,2,1,0:T(8,128)(2,1)S(1)}, bf16[8,2,128,128]{3,2,1,0:T(8,128)(2,1)S(1)}, u32[]{:S(2)}, u32[]{:S(2)}) collective-permute-start(bf16[8,2,128,128]{3,2,1,0:T(8,128)(2,1)S(1)} %add_parts.1), channel_id=1, source_target_pairs={{0,24},{8,0},{16,8},{24,16},{1,25},{9,1},{17,9},{25,17},{2,26},{10... | collective-permute-start | bytes 1572872 | tf_op jit(solution)/shard_map/ppermute | solution.py:535
  178.5 34.7 %all-to-all-start.4 = ((bf16[8,4,128,128]{3,2,1,0:T(8,128)(2,1)}), bf16[8,4,128,128]{3,2,1,0:T(8,128)(2,1)S(1)}, u32[]{:S(2)}, u32[]{:S(2)}) async-start(bf16[8,4,128,128]{3,2,1,0:T(8,128)(2,1)} %collect.1), calls=%async_computation.4 | async-start | bytes 2097152 | tf_op jit(solution)/shard_map/all_to_all | solution.py:466
  213.2 1.0 copy-start.2
  214.1 58.7 %all-to-all-start.5 = ((bf16[32,2,128,128]{3,2,1,0:T(8,128)(2,1)}), bf16[32,2,128,128]{3,2,1,0:T(8,128)(2,1)S(1)}, u32[]{:S(2)}, u32[]{:S(2)}) async-start(bf16[32,2,128,128]{3,2,1,0:T(8,128)(2,1)} %get-tuple-element.60), calls=%async_computation.5 | async-start | bytes 4194304 | tf_op jit(solution)/shard_map/all_to_all | solution.py:466
  272.8 1.3 copy-start.3
  274.1 61.5 %all-to-all-start.6 = ((bf16[32,288,128]{2,1,0:T(8,128)(2,1)}), bf16[32,288,128]{2,1,0:T(8,128)(2,1)S(1)}, u32[]{:S(2)}, u32[]{:S(2)}) async-start(bf16[32,288,128]{2,1,0:T(8,128)(2,1)} %share_rows.1), calls=%async_computation.6 | async-start | bytes 4718592 | tf_op jit(solution)/shard_map/all_to_all | solution.py:466
  335.7 1.4 copy-start.1
where the time goes:
time: 354 us; the launch traced here: 347 us
  waiting for transfers between devices  119 us (34%)
  Pallas kernels  93.2 us (26%)
  blocking collectives  61.6 us (17%)
  starting transfers between devices  59.6 us (17%)
  local copies, waits for them, and re-layouts  6.79 us (2%)
  between operations  5.01 us (1%)
    pallas_call x9, Pallas kernels, run(): pl.pallas_call(body, out_shape=tuple((jax.ShapeDtypeStruct(*o) for o in o...  87.7 us
    ppermute x7, waiting for transfers between devices, shift(): return lax.ppermute(values, 'x', [(x, (x + s) % n_x) for x in range(n_x)])  62.5 us
    all_to_all x6, waiting for transfers between devices, swap(): return lax.all_to_all(values, axes, split_axis=0, concat_axis=0, tiled=True)  56.6 us
    all_to_all x6, starting transfers between devices, swap(): return lax.all_to_all(values, axes, split_axis=0, concat_axis=0, tiled=True)  51.5 us
    all_to_all x1, blocking collectives, swap(): return lax.all_to_all(values, axes, split_axis=0, concat_axis=0, tiled=True)  34.6 us
    all_gather x1, blocking collectives, shards(): lax.all_gather(jnp.stack([gain_q, gain_k]), 'fsdp', axis=1, tiled=True)  13.8 us
    psum x1, blocking collectives, shards(): gain_sums = lax.psum(jnp.concatenate([gain_main, gain_extra]), 'fsdp')  13.3 us
    ppermute x7, starting transfers between devices, shift(): return lax.ppermute(values, 'x', [(x, (x + s) % n_x) for x in range(n_x)])  8.15 us
  transfers between devices with their start and end apart: 13, of which 8 were waited for; matrix products, arithmetic and copies ran while one was open for 1% of the time, Pallas kernels for 23%

commit v1 on v0

--- a/solution.py
+++ b/solution.py
@@ -58,7 +58,7 @@
         writes[o].wait()
 
 
-def call(kernel, name, outs, in_specs, tiles_moved, flops=0, scratch=(), smem_outs=(), hbm_in=(), hbm_out=(), lazy=False, room=vmem_bytes):
+def call(kernel, name, outs, in_specs, tiles_moved, flops=0, scratch=(), smem_outs=(), hbm_in=(), hbm_out=(), lazy=False):
     def run(*operands):
         specs = [hbm if i in hbm_in else spec for i, spec in enumerate(in_specs)]
         kinds = (smem if n in smem_outs else hbm if n in hbm_out else vmem for n in range(len(outs)))
@@ -75,7 +75,7 @@
             out_specs=tuple(kinds),
             scratch_shapes=[*scratch, *extra],
             compiler_params=pltpu.CompilerParams(
-                vmem_limit_bytes=most_vmem if buffers else room
+                vmem_limit_bytes=most_vmem if buffers else vmem_bytes
             ),
             cost_estimate=pl.CostEstimate(
                 flops=flops, bytes_accessed=tiles_moved * tile_rows * head_width * 2, transcendentals=0
@@ -162,7 +162,9 @@
         grad_v_ref[:, at] = main_ref[p, 1] if p < n_seq else extra_ref[p - n_seq, 3]
 
 
-def back_kernel(n_seq, heads, order_ref, main_ref, extra_ref, q_ref, k_ref, gain_ref, gq_ref, gk_ref, ready, flush):
+def back_kernel(n_x, n_z, heads, per, order_ref, main_ref, extra_ref, q_ref, k_ref, gain_ref, *refs, ready, flush):
+    n_seq = n_x * n_z
+    finish_in, (gq_ref, gk_ref), finish_out = refs[:5], refs[5:7], refs[7:]
     ready(2)
     ready(1)
     scale = 1.0 / (heads * head_width)
@@ -189,6 +191,7 @@
             at, x, weighted = pieces(p)
             out_ref[:, at] = (inverse * weighted - x * pull).astype(bf16)
         flush(which)
+    finish(n_x, n_z, heads, per, order_ref, main_ref, *finish_in, *finish_out)
 
 
 def fold_rows(values, combine):
@@ -405,14 +408,12 @@
         copy.wait()
 
 
-def finish_kernel(n_x, n_z, heads, per, order_ref, slot_ref, here_ref, lse_ref, gq_ref, gk_ref, home_hbm, out_ref, sq_ref, sk_ref, rows_ref, shared_ref, held_ref, sem):
+def finish(n_x, n_z, heads, per, order_ref, home_ref, slot_ref, here_ref, lse_ref, gq_ref, gk_ref, out_ref, sq_ref, sk_ref, shared_ref, held_ref):
     n_seq = n_x * n_z
     own, f_index = here_ref[0], here_ref[1]
-    last = pl.ds(home_hbm.shape[1] - shared_rows, shared_rows)
-    copy = pltpu.make_async_copy(home_hbm.at[:, last], rows_ref, sem)
-    copy.start()
-    copy.wait()
-    shared_ref[...] = rows_ref[...].astype(f32)
+    last = pl.ds(home_ref.shape[1] - shared_rows, shared_rows)
+    for d in range(n_seq):
+        shared_ref[d] = home_ref[d, last].astype(f32)
 
     def row(device, line):
         lines = [8 * t + line for t in range(1, 4)] if line < n_z else [line - n_z, line - n_z + 4]
@@ -647,39 +648,38 @@
         hbm_in=(1, 2),
         hbm_out=(0, 1),
     )(order, odv_home, extra_home)
-    grad_q, grad_k = call(
-        functools.partial(back_kernel, n_seq, heads),
+    per = heads // n_f
+    grad_q, grad_k, lse_slots, share_q, share_k = call(
+        functools.partial(back_kernel, n_x, n_z, heads, per),
         "gradients_home",
-        [wide, wide],
-        [smem] + [vmem] * 5,
+        [
+            wide,
+            wide,
+            ((2, n_tiles * tile_rows), f32),
+            ((per, head_width), f32),
+            ((per, head_width), f32),
+        ],
+        [smem] + [vmem] * 5 + [smem] * 2 + [vmem] * 3,
         6 * heads,
+        scratch=[
+            pltpu.VMEM((n_seq, shared_rows, head_width), f32),
+            pltpu.VMEM((2, n_tiles, tile_rows), f32),
+        ],
         hbm_in=(2, 1, 3, 4),
         hbm_out=(0, 1),
         lazy=True,
-    )(order, dqk_home, extra_home, q2, k2, gains)
-
-    per = heads // n_f
-    lse_slots, share_q, share_k = call(
-        functools.partial(finish_kernel, n_x, n_z, heads, per),
-        "finish",
-        [((2, n_tiles * tile_rows), f32), ((per, head_width), f32), ((per, head_width), f32)],
-        [smem] * 3 + [vmem] * 3 + [hbm],
-        32,
-        scratch=[
-            pltpu.VMEM((n_seq, shared_rows, head_width), bf16),
-            pltpu.VMEM((n_seq, shared_rows, head_width), f32),
-            pltpu.VMEM((2, n_tiles, tile_rows), f32),
-            pltpu.SemaphoreType.DMA,
-        ],
-        room=most_vmem,
     )(
         order,
+        dqk_home,
+        extra_home,
+        q2,
+        k2,
+        gains,
         head_slot,
         jnp.stack([own, f_index]),
         lse_main,
         gain_q.reshape(per, head_width),
         gain_k.reshape(per, head_width),
-        dqk_home,
     )
     whole = lambda a: a.reshape(1, tile_rows, features)
     return (

time: 354 us -> 354 us (level)
  waiting for transfers between devices: 119 us -> 115 us
    all_to_all x6, waiting for transfers between devices: 56.6 us -> 52.8 us  [swap(): return lax.all_to_all(values, axes, split_axis=0, concat_axis=0, tiled=True)]
    pallas_call x9 -> x8, Pallas kernels: 87.7 us -> 90.7 us  [run(): pl.pallas_call(body, out_shape=tuple((jax.ShapeDtypeStruct(*o) for o in o...]
  transfers between devices with their start and end apart: 13 -> 13, of which waited for: 8 -> 7; matrix products, arithmetic and copies ran while one was open for 1% -> 1% of each run, Pallas kernels for 23% -> 24%
where the time goes in v1:
time: 354 us; the launch traced here: 349 us
  waiting for transfers between devices  115 us (32%)
  Pallas kernels  96.2 us (27%)
  starting transfers between devices  61.9 us (17%)
  blocking collectives  61.9 us (17%)
  local copies, waits for them, and re-layouts  6.8 us (2%)
  between operations  5.01 us (1%)
    pallas_call x8, Pallas kernels, run(): pl.pallas_call(body, out_shape=tuple((jax.ShapeDtypeStruct(*o) for o in o...  90.7 us
    ppermute x7, waiting for transfers between devices, shift(): return lax.ppermute(values, 'x', [(x, (x + s) % n_x) for x in range(n_x)])  62.5 us
    all_to_all x6, starting transfers between devices, swap(): return lax.all_to_all(values, axes, split_axis=0, concat_axis=0, tiled=True)  53.8 us
    all_to_all x6, waiting for transfers between devices, swap(): return lax.all_to_all(values, axes, split_axis=0, concat_axis=0, tiled=True)  52.8 us
    all_to_all x1, blocking collectives, swap(): return lax.all_to_all(values, axes, split_axis=0, concat_axis=0, tiled=True)  34.5 us
    all_gather x1, blocking collectives, shards(): lax.all_gather(jnp.stack([gain_q, gain_k]), 'fsdp', axis=1, tiled=True)  13.8 us
    psum x1, blocking collectives, shards(): gain_sums = lax.psum(jnp.concatenate([gain_main, gain_extra]), 'fsdp')  13.6 us
    ppermute x7, starting transfers between devices, shift(): return lax.ppermute(values, 'x', [(x, (x + s) % n_x) for x in range(n_x)])  8.18 us
  transfers between devices with their start and end apart: 13, of which 7 were waited for; matrix products, arithmetic and copies ran while one was open for 1% of the time, Pallas kernels for 24%

profile of v1, /device:TPU:4, one launch (start us, length us, event | category | flops | bytes accessed | tf_op | source)
XLA Modules:
  0.0 348.6 jit_solution(11677388771339076125)
XLA Ops:
  0.6 3.7 %place_heads.1 = (s32[80]{0:T(128)}, bf16[32,128,128]{2,1,0:T(8,128)(2,1)}) custom-call(s32[40]{0:T(128)} %refs_6_.1, bf16[128,5120]{1,0:T(8,128)(2,1)} %bitcast.20), custom_call_target="tpu_custom_call" | custom-call | tf_op jit(solution)/shard_map/place_heads/pallas_call | solution.py:469
  4.4 11.7 %all-to-all-start = ((bf16[32,128,128]{2,1,0:T(8,128)(2,1)}), bf16[32,128,128]{2,1,0:T(8,128)(2,1)S(1)}, u32[]{:S(2)}, u32[]{:S(2)}) async-start(bf16[32,128,128]{2,1,0:T(8,128)(2,1)} %get-tuple-element.45), calls=%async_computation | async-start | bytes 2097152 | tf_op jit(solution)/shard_map/all_to_all | solution.py:467
  22.3 13.8 %all_gather.3.refs_5_ = bf16[2,5120]{1,0:T(2,128)(2,1)} all-gather(bf16[2,640]{1,0:T(2,128)(2,1)S(1)} %pad_maximum_fusion), channel_id=1, replica_groups=mesh['z'=8,'x'=4,'fsdp'=8] {'fsdp'}, dimensions={1}, use_global_device_ids=true | all-gather | bytes 23040 | tf_op jit(solution)/shard_map/all_gather | solution.py:488
  36.1 6.7 %normalize.1 = (bf16[32,2,128,128]{3,2,1,0:T(8,128)(2,1)}, bf16[32,128,128]{2,1,0:T(8,128)(2,1)}, bf16[8,4,128,128]{3,2,1,0:T(8,128)(2,1)}) custom-call(s32[80]{0:T(128)} %get-tuple-element.41.refs_0_, bf16[128,5120]{1,0:T(8,128)(2,1)} %bitcast.22, bf16[128,5120]{1,0:T(8,128)(2,1)} %bitcast.24, bf16[128,5120]{1,0:T(8,128)(2,1)} %bitcast.21, ...), custom_call_target="tpu_custom_call" | custom-call | bytes 9175040 | tf_op jit(solution)/shard_map/normalize/pallas_call | solution.py:71
  42.9 1.3 all-to-all-done.refs_2_
  44.2 1.0 copy-done.4
  45.2 34.5 %all_to_all.35.refs_1_ = bf16[8,4,128,128]{3,2,1,0:T(8,128)(2,1)S(1)} all-to-all(bf16[8,4,128,128]{3,2,1,0:T(8,128)(2,1)} %get-tuple-element.46), channel_id=1, replica_groups=mesh['z'=8,'x'=4,'fsdp'=8] {'z'}, dimensions={0} | all-to-all | bytes 2097152 | tf_op jit(solution)/shard_map/all_to_all | solution.py:467
  79.7 5.0 %all-to-all-start.2 = ((bf16[32,128,128]{2,1,0:T(8,128)(2,1)}), bf16[32,128,128]{2,1,0:T(8,128)(2,1)}, u32[]{:S(2)}, u32[]{:S(2)}) async-start(bf16[32,128,128]{2,1,0:T(8,128)(2,1)} %get-tuple-element.47), calls=%async_computation.2 | async-start | bytes 2097152 | tf_op jit(solution)/shard_map/all_to_all | solution.py:467
  85.4 1.5 collective-permute-start
  86.9 21.8 %collective-permute-done.2.refs_5_ = bf16[8,2,128,128]{3,2,1,0:T(8,128)(2,1)S(1)} collective-permute-done((bf16[8,2,128,128]{3,2,1,0:T(8,128)(2,1)S(1)}, bf16[8,2,128,128]{3,2,1,0:T(8,128)(2,1)S(1)}, u32[]{:S(2)}, u32[]{:S(2)}) %collective-permute-start.2) | collective-permute-done | bytes 524320 | tf_op jit(solution)/shard_map/ppermute | solution.py:536
  109.0 2.0 collective-permute-start.1
  110.9 5.7 %collective-permute-done.3.refs_4_ = bf16[4,2,128,128]{3,2,1,0:T(8,128)(2,1)S(1)} collective-permute-done((bf16[4,2,128,128]{3,2,1,0:T(8,128)(2,1)S(1)}, bf16[4,2,128,128]{3,2,1,0:T(8,128)(2,1)S(1)}, u32[]{:S(2)}, u32[]{:S(2)}) %collective-permute-start.3) | collective-permute-done | bytes 262176 | tf_op jit(solution)/shard_map/ppermute | solution.py:536
  116.7 11.1 %all-to-all-start.3 = ((bf16[32,2,128,128]{3,2,1,0:T(8,128)(2,1)}), bf16[32,2,128,128]{3,2,1,0:T(8,128)(2,1)}, u32[]{:S(2)}, u32[]{:S(2)}) async-start(bf16[32,2,128,128]{3,2,1,0:T(8,128)(2,1)} %get-tuple-element.48), calls=%async_computation.3 | async-start | bytes 4194304 | tf_op jit(solution)/shard_map/all_to_all | solution.py:467
  127.8 10.3 %attention_second.1 = (bf16[8,2,128,128]{3,2,1,0:T(8,128)(2,1)S(1)}, f32[8,128]{1,0:T(8,128)S(1)}, f32[2,128]{1,0:T(2,128)S(1)}, bf16[8,2,128,128]{3,2,1,0:T(8,1...) custom-call(s32[97]{0:T(128)S(1)} %pad_add_fusion.refs_0_, ...), custom_call_target="tpu_custom_call" | custom-call | flops 7381975040 | bytes 10485760 | tf_op jit(solution)/shard_map/attention_second/pallas_call | solution.py:71
  138.7 1.5 collective-permute-start.4
  140.2 19.2 %collective-permute-done.5.two_ref = bf16[8,2,128,128]{3,2,1,0:T(8,128)(2,1)S(1)} collective-permute-done((bf16[8,2,128,128]{3,2,1,0:T(8,128)(2,1)S(1)}, bf16[8,2,128,128]{3,2,1,0:T(8,128)(2,1)S(1)}, u32[]{:S(2)}, u32[]{:S(2)}) %collective-permute-start.5) | collective-permute-done | bytes 524320 | tf_op jit(solution)/shard_map/ppermute | solution.py:536
  159.5 1.8 collective-permute-start.6
  161.3 15.8 %collective-permute-done.6.refs_2_ = bf16[8,2,128,128]{3,2,1,0:T(8,128)(2,1)S(1)} collective-permute-done((bf16[8,2,128,128]{3,2,1,0:T(8,128)(2,1)S(1)}, bf16[8,2,128,128]{3,2,1,0:T(8,128)(2,1)S(1)}, u32[]{:S(2)}, u32[]{:S(2)}) %collective-permute-start.6) | collective-permute-done | bytes 524320 | tf_op jit(solution)/shard_map/ppermute | solution.py:536
  177.1 1.2 collect.1
  178.4 6.8 %all-to-all-start.4 = ((bf16[8,4,128,128]{3,2,1,0:T(8,128)(2,1)}), bf16[8,4,128,128]{3,2,1,0:T(8,128)(2,1)S(1)}, u32[]{:S(2)}, u32[]{:S(2)}) async-start(bf16[8,4,128,128]{3,2,1,0:T(8,128)(2,1)} %collect.1), calls=%async_computation.4 | async-start | bytes 2097152 | tf_op jit(solution)/shard_map/all_to_all | solution.py:467
  185.1 29.1 %forward_first.1 = (bf16[32,2,128,128]{3,2,1,0:T(8,128)(2,1)}, f32[32,128]{1,0:T(8,128)}, f32[32,128]{1,0:T(8,128)}) custom-call(s32[384]{0:T(512)} %reshape.63.refs_0_, bf16[32,2,128,128]{3,2,1,0:T(8,128)(2,1)} %all-to-all-done.3.refs_1_, bf16[32,128,128]{2,1,0:T(8,128)(2,1)} %copy-done.4, bf16[32,128,128]{2,1,0:T(8,128)(2,1)} %all-to-all-done.2.refs_3_), custom_call_target="tpu_custom_call" | custom-call | flops 14763950080 | bytes 10485760 | tf_op jit(solution)/shard_map/forward_first/pallas_call | solution.py:71
  215.3 10.8 %all-to-all-start.5 = ((bf16[32,2,128,128]{3,2,1,0:T(8,128)(2,1)}), bf16[32,2,128,128]{3,2,1,0:T(8,128)(2,1)S(1)}, u32[]{:S(2)}, u32[]{:S(2)}) async-start(bf16[32,2,128,128]{3,2,1,0:T(8,128)(2,1)} %get-tuple-element.60), calls=%async_computation.5 | async-start | bytes 4194304 | tf_op jit(solution)/shard_map/all_to_all | solution.py:467
  226.1 30.6 %backward_first.1 = (bf16[32,288,128]{2,1,0:T(8,128)(2,1)}, f32[2,128]{1,0:T(2,128)}) custom-call(s32[384]{0:T(512)} %reshape.63.refs_0_, bf16[32,2,128,128]{3,2,1,0:T(8,128)(2,1)} %all-to-all-done.3.refs_1_, bf16[32,128,128]{2,1,0:T(8,128)(2,1)} %copy-done.4, bf16[32,128,128]{2,1,0:T(8,128)(2,1)} %all-to-all-done.2.refs_3_, ...), custom_call_target="tpu_custom_call" | custom-call | flops 23622320128 | bytes 10485760 | tf_op jit(solution)/shard_map/backward_first/pallas_call | solution.py:71
  257.4 13.6 %psum.7.sums_ref = f32[4,128]{1,0:T(4,128)} all-reduce(f32[4,128]{1,0:T(4,128)S(1)} %pad_maximum_fusion.1), channel_id=1, replica_groups=mesh['z'=8,'x'=4,'fsdp'=8] {'fsdp'}, use_global_device_ids=true, to_apply=%region_0.1 | all-reduce | flops 512 | bytes 4096 | tf_op jit(solution)/shard_map/psum | solution.py:623
  271.0 1.8 share_rows.1
  272.7 1.8 all-to-all-done.5.refs_1_
  274.5 1.3 copy-done.3
  275.9 8.3 %all-to-all-start.6 = ((bf16[32,288,128]{2,1,0:T(8,128)(2,1)}), bf16[32,288,128]{2,1,0:T(8,128)(2,1)S(1)}, u32[]{:S(2)}, u32[]{:S(2)}) async-start(bf16[32,288,128]{2,1,0:T(8,128)(2,1)} %share_rows.1), calls=%async_computation.6 | async-start | bytes 4718592 | tf_op jit(solution)/shard_map/all_to_all | solution.py:467
  284.7 4.8 %merge_heads.1 = (bf16[128,5120]{1,0:T(8,128)(2,1)}, bf16[128,5120]{1,0:T(8,128)(2,1)}) custom-call(s32[80]{0:T(128)} %get-tuple-element.41.refs_0_, bf16[32,2,128,128]{3,2,1,0:T(8,128)(2,1)} %copy-done.3, bf16[8,4,128,128]{3,2,1,0:T(8,128)(2,1)} %copy-done.2), custom_call_target="tpu_custom_call" | custom-call | bytes 5242880 | tf_op jit(solution)/shard_map/merge_heads/pallas_call | solution.py:71
  289.5 49.6 %all-to-all-done.6.refs_1_ = bf16[32,288,128]{2,1,0:T(8,128)(2,1)S(1)} async-done(((bf16[32,288,128]{2,1,0:T(8,128)(2,1)}), bf16[32,288,128]{2,1,0:T(8,128)(2,1)S(1)}, u32[]{:S(2)}, u32[]{:S(2)}) %all-to-all-start.6) | async-done | bytes 2359328 | tf_op jit(solution)/shard_map/all_to_all | solution.py:467
  339.1 1.4 copy-done.1
  340.6 7.8 %gradients_home.1 = (bf16[128,5120]{1,0:T(8,128)(2,1)}, bf16[128,5120]{1,0:T(8,128)(2,1)}, f32[2,4096]{1,0:T(2,128)}, f32[5,128]{1,0:T(8,128)}, f32[5,128]{1,0:T(8,128)}) custom-call(s32[80]{0:T(128)} %get-tuple-element.41.refs_0_, bf16[32,288,128]{2,1,0:T(8,128)(2,1)} %copy-done.1, bf16[8,4,128,128]{3,2,1,0:T(8,128)(2,1)} %copy-done.2, ...), custom_call_target="tpu_custom_call" | custom-call | bytes 7864320 | tf_op jit(solution)/shard_map/gradients_home/pallas_call | solution.py:71
  (43 shorter events, 6.3 us)
Async XLA Ops:
  4.4 11.8 %copy-start.7 = (s32[80]{0:T(128)S(1)}, s32[80]{0:T(128)}, u32[]{:S(2)}) copy-start(s32[80]{0:T(128)} %get-tuple-element.41.refs_0_) | copy-start | bytes 964
  4.4 15.0 %copy-start.9 = (bf16[640]{0:T(1024)(128)(2,1)S(1)}, bf16[640]{0:T(1024)(128)(2,1)}, u32[]{:S(2)}) copy-start(bf16[640]{0:T(1024)(128)(2,1)} %param.13) | copy-start | bytes 3844
  4.4 15.0 %copy-start.8 = (bf16[640]{0:T(1024)(128)(2,1)S(1)}, bf16[640]{0:T(1024)(128)(2,1)}, u32[]{:S(2)}) copy-start(bf16[640]{0:T(1024)(128)(2,1)} %param.14) | copy-start | bytes 3844
  4.4 16.3 %copy-start.5 = (s32[40,32,11]{0,1,2:T(8,128)S(1)}, s32[40,32,11]{0,1,2:T(8,128)}, u32[]{:S(2)}) copy-start(s32[40,32,11]{0,1,2:T(8,128)} %param.15) | copy-start | bytes 168964
  4.4 16.3 %copy-start.6 = (s32[40,32]{0,1:T(8,128)S(1)}, s32[40,32]{0,1:T(8,128)}, u32[]{:S(2)}) copy-start(s32[40,32]{0,1:T(8,128)} %param.16) | copy-start | bytes 15364
  4.4 39.8 %all-to-all-start = ((bf16[32,128,128]{2,1,0:T(8,128)(2,1)}), bf16[32,128,128]{2,1,0:T(8,128)(2,1)S(1)}, u32[]{:S(2)}, u32[]{:S(2)}) async-start(bf16[32,128,128]{2,1,0:T(8,128)(2,1)} %get-tuple-element.45), calls=%async_computation | async-start | bytes 2097152 | tf_op jit(solution)/shard_map/all_to_all | solution.py:467
  44.2 1.0 copy-start.4
  79.7 36.9 %all-to-all-start.2 = ((bf16[32,128,128]{2,1,0:T(8,128)(2,1)}), bf16[32,128,128]{2,1,0:T(8,128)(2,1)}, u32[]{:S(2)}, u32[]{:S(2)}) async-start(bf16[32,128,128]{2,1,0:T(8,128)(2,1)} %get-tuple-element.47), calls=%async_computation.2 | async-start | bytes 2097152 | tf_op jit(solution)/shard_map/all_to_all | solution.py:467
  84.8 23.9 %collective-permute-start.2 = (bf16[8,2,128,128]{3,2,1,0:T(8,128)(2,1)S(1)}, bf16[8,2,128,128]{3,2,1,0:T(8,128)(2,1)S(1)}, u32[]{:S(2)}, u32[]{:S(2)}) collective-permute-start(bf16[8,2,128,128]{3,2,1,0:T(8,128)(2,1)S(1)} %slice.12), channel_id=1, source_target_pairs={{0,24},{8,0},{16,8},{24,16},{1,25},{9,1},{17,9},{25,17},{2,26},{10... | collective-permute-start | bytes 1572872 | tf_op jit(solution)/shard_map/ppermute | solution.py:536
  85.4 23.5 %collective-permute-start = (bf16[8,2,128,128]{3,2,1,0:T(8,128)(2,1)S(1)}, bf16[8,2,128,128]{3,2,1,0:T(8,128)(2,1)S(1)}, u32[]{:S(2)}, u32[]{:S(2)}) collective-permute-start(bf16[8,2,128,128]{3,2,1,0:T(8,128)(2,1)S(1)} %slice.12), channel_id=1, source_target_pairs={{0,8},{8,16},{16,24},{24,0},{1,9},{9,17},{17,25},{25,1},{2,10},{10... | collective-permute-start | bytes 1572872 | tf_op jit(solution)/shard_map/ppermute | solution.py:536
  108.7 7.9 %collective-permute-start.3 = (bf16[4,2,128,128]{3,2,1,0:T(8,128)(2,1)S(1)}, bf16[4,2,128,128]{3,2,1,0:T(8,128)(2,1)S(1)}, u32[]{:S(2)}, u32[]{:S(2)}) collective-permute-start(bf16[4,2,128,128]{3,2,1,0:T(8,128)(2,1)S(1)} %slice.14), channel_id=1, source_target_pairs={{0,24},{8,0},{16,8},{24,16},{1,25},{9,1},{17,9},{25,17},{2,26},{10... | collective-permute-start | bytes 786440 | tf_op jit(solution)/shard_map/ppermute | solution.py:536
  109.0 7.7 %collective-permute-start.1 = (bf16[4,2,128,128]{3,2,1,0:T(8,128)(2,1)S(1)}, bf16[4,2,128,128]{3,2,1,0:T(8,128)(2,1)S(1)}, u32[]{:S(2)}, u32[]{:S(2)}) collective-permute-start(bf16[4,2,128,128]{3,2,1,0:T(8,128)(2,1)S(1)} %slice.13), channel_id=1, source_target_pairs={{0,8},{8,16},{16,24},{24,0},{1,9},{9,17},{17,25},{25,1},{2,10},{10... | collective-permute-start | bytes 786440 | tf_op jit(solution)/shard_map/ppermute | solution.py:536
  116.7 61.7 %all-to-all-start.3 = ((bf16[32,2,128,128]{3,2,1,0:T(8,128)(2,1)}), bf16[32,2,128,128]{3,2,1,0:T(8,128)(2,1)}, u32[]{:S(2)}, u32[]{:S(2)}) async-start(bf16[32,2,128,128]{3,2,1,0:T(8,128)(2,1)} %get-tuple-element.48), calls=%async_computation.3 | async-start | bytes 4194304 | tf_op jit(solution)/shard_map/all_to_all | solution.py:467
  138.1 39.1 %copy-start = (f32[8,128]{1,0:T(8,128)}, f32[8,128]{1,0:T(8,128)S(1)}, u32[]{:S(2)}) copy-start(f32[8,128]{1,0:T(8,128)S(1)} %get-tuple-element.66.lse_ref) | copy-start | bytes 12292
  138.1 21.3 %collective-permute-start.5 = (bf16[8,2,128,128]{3,2,1,0:T(8,128)(2,1)S(1)}, bf16[8,2,128,128]{3,2,1,0:T(8,128)(2,1)S(1)}, u32[]{:S(2)}, u32[]{:S(2)}) collective-permute-start(bf16[8,2,128,128]{3,2,1,0:T(8,128)(2,1)S(1)} %get-tuple-element.58), channel_id=1, source_target_pairs={{0,24},{8,0},{16,8},{24,16},{1,25},{9,1},{17,9},{25,17},{2,26},{10... | collective-permute-start | bytes 1572872 | tf_op jit(solution)/shard_map/ppermute | solution.py:536
  138.7 22.6 %collective-permute-start.4 = (bf16[8,2,128,128]{3,2,1,0:T(8,128)(2,1)S(1)}, bf16[8,2,128,128]{3,2,1,0:T(8,128)(2,1)S(1)}, u32[]{:S(2)}, u32[]{:S(2)}) collective-permute-start(bf16[8,2,128,128]{3,2,1,0:T(8,128)(2,1)S(1)} %get-tuple-element.56), channel_id=1, source_target_pairs={{0,8},{8,16},{16,24},{24,0},{1,9},{9,17},{17,25},{25,1},{2,10},{10... | collective-permute-start | bytes 1572872 | tf_op jit(solution)/shard_map/ppermute | solution.py:536
  159.5 17.6 %collective-permute-start.6 = (bf16[8,2,128,128]{3,2,1,0:T(8,128)(2,1)S(1)}, bf16[8,2,128,128]{3,2,1,0:T(8,128)(2,1)S(1)}, u32[]{:S(2)}, u32[]{:S(2)}) collective-permute-start(bf16[8,2,128,128]{3,2,1,0:T(8,128)(2,1)S(1)} %add_parts.1), channel_id=1, source_target_pairs={{0,24},{8,0},{16,8},{24,16},{1,25},{9,1},{17,9},{25,17},{2,26},{10... | collective-permute-start | bytes 1572872 | tf_op jit(solution)/shard_map/ppermute | solution.py:536
  178.4 35.9 %all-to-all-start.4 = ((bf16[8,4,128,128]{3,2,1,0:T(8,128)(2,1)}), bf16[8,4,128,128]{3,2,1,0:T(8,128)(2,1)S(1)}, u32[]{:S(2)}, u32[]{:S(2)}) async-start(bf16[8,4,128,128]{3,2,1,0:T(8,128)(2,1)} %collect.1), calls=%async_computation.4 | async-start | bytes 2097152 | tf_op jit(solution)/shard_map/all_to_all | solution.py:467
  214.3 1.0 copy-start.2
  215.3 59.3 %all-to-all-start.5 = ((bf16[32,2,128,128]{3,2,1,0:T(8,128)(2,1)}), bf16[32,2,128,128]{3,2,1,0:T(8,128)(2,1)S(1)}, u32[]{:S(2)}, u32[]{:S(2)}) async-start(bf16[32,2,128,128]{3,2,1,0:T(8,128)(2,1)} %get-tuple-element.60), calls=%async_computation.5 | async-start | bytes 4194304 | tf_op jit(solution)/shard_map/all_to_all | solution.py:467
  274.5 1.3 copy-start.3
  275.9 63.3 %all-to-all-start.6 = ((bf16[32,288,128]{2,1,0:T(8,128)(2,1)}), bf16[32,288,128]{2,1,0:T(8,128)(2,1)S(1)}, u32[]{:S(2)}, u32[]{:S(2)}) async-start(bf16[32,288,128]{2,1,0:T(8,128)(2,1)} %share_rows.1), calls=%async_computation.6 | async-start | bytes 4718592 | tf_op jit(solution)/shard_map/all_to_all | solution.py:467
  339.1 1.4 copy-start.1
